TPU v7x, 32 devices: a whole 2x2x4 slice. The times are simulated.
32 devices in a mesh: grp: 2 (over x), chan: 16 (over z, y, core).
Axes of the slice: x: 2, y: 2, z: 4, core: 2. Of those that a mesh axis runs over, the one named last changes fastest.
Arguments:
- voltages_real: int32 [256, 32, 1024], P('chan', 'grp'), parts along dimension 1, may hold values from -127 to 127, as said below
- voltages_imag: int32 [256, 32, 1024], P('chan', 'grp'), parts along dimension 1, may hold values from -127 to 127, as said below
- model: bfloat16 [2, 128, 4608], replicated, may hold values from -10 to 10
- gains: float32 [2, 2048], P(None, 'grp'), parts along dimension 1, may hold values from -2.5 to 2.5
- bandpass: float32 [32], P(('grp', 'chan')), parts along dimension 0, may hold values from 0.3 to 3.3
Outputs:
- residual: float32 [32, 2, 128, 4608], P(('grp', 'chan')), parts along dimension 0
- new_gains: float32 [2, 2048], P(None, ('grp', 'chan')), parts along dimension 1
There are 2 independent parts, one for each index of `grp`. A program takes and returns all parts, laid end to end along the dimension named above; an argument that names none is the same for every part. Nothing has to cross between parts.
Inputs may be any that keep to these rules, and one draw needn't show every extreme that they name: `voltages_real`: quantized voltage components, saturated symmetrically at -127 and 127. `voltages_imag`: quantized voltage components, saturated symmetrically at -127 and 127.
All inputs are finite; a program needn't handle non-finite values.
Results may differ from a plain program's by a relative error of at most 0.0003.
Values may be sent and summed in bfloat16 or wider, within the bound.
A program may use at most 128 MiB of HBM per device.

v0:
```python
import jax
import jax.numpy as jnp
from jax import lax
from jax.sharding import PartitionSpec as P


def strip_product(first, second, stripe, tile_width):
    row_part = first[:, :, stripe * tile_width : (stripe + 1) * tile_width]
    col_part = second[:, :, : (stripe + 1) * tile_width]
    return jnp.einsum("scr,scn->crn", row_part, col_part, preferred_element_type=jnp.float32)


def strip_terms(q_real, q_imag, gain_real, gain_imag, stripe, tile_width, input_count):
    start = stripe * tile_width
    span = (stripe + 1) * tile_width
    col_real = gain_real[:span]
    col_imag = gain_imag[:span]
    own_real = gain_real[start:span]
    own_imag = gain_imag[start:span]
    f32 = jnp.float32
    row_re = jnp.einsum("crn,n->r", q_real, col_real, preferred_element_type=f32) - jnp.einsum(
        "crn,n->r", q_imag, col_imag, preferred_element_type=f32
    )
    row_im = jnp.einsum("crn,n->r", q_real, col_imag, preferred_element_type=f32) + jnp.einsum(
        "crn,n->r", q_imag, col_real, preferred_element_type=f32
    )
    col_re = jnp.einsum("r,crn->n", own_real, q_real, preferred_element_type=f32) + jnp.einsum(
        "r,crn->n", own_imag, q_imag, preferred_element_type=f32
    )
    col_im = jnp.einsum("r,crn->n", own_imag, q_real, preferred_element_type=f32) - jnp.einsum(
        "r,crn->n", own_real, q_imag, preferred_element_type=f32
    )
    total_real = (
        jnp.zeros((input_count,), jnp.float32).at[:span].add(col_re).at[start:span].add(row_re)
    )
    total_imag = (
        jnp.zeros((input_count,), jnp.float32).at[:span].add(col_im).at[start:span].add(row_im)
    )
    return jnp.stack([total_real, total_imag])


def shards(voltages_real, voltages_imag, model, gains, bandpass):
    tile_width = model.shape[1]
    input_count = gains.shape[1]
    block_count = input_count // tile_width
    sample_total = voltages_real.shape[0] * lax.axis_size("chan")
    scale_factor = 1.0 / (4096.0 * sample_total)
    real_send = voltages_real.astype(jnp.bfloat16)
    imag_send = voltages_imag.astype(jnp.bfloat16)
    grams = []
    real_own, imag_own = (
        lax.all_to_all(real_send, "chan", split_axis=1, concat_axis=0, tiled=True),
        lax.all_to_all(imag_send, "chan", split_axis=1, concat_axis=0, tiled=True),
    )
    left_side = jnp.concatenate([real_own, imag_own], axis=0)
    swapped = jnp.concatenate([-imag_own, real_own], axis=0)
    for stripe in range(block_count):
        grams.append(
            (
                strip_product(left_side, left_side, stripe, tile_width),
                strip_product(left_side, swapped, stripe, tile_width),
            )
        )
    gain_real = gains[0]
    gain_imag = gains[1]
    short_real = gain_real.astype(jnp.bfloat16)
    short_imag = gain_imag.astype(jnp.bfloat16)
    power_gain = gain_real * gain_real + gain_imag * gain_imag
    band_column = bandpass[:, None, None]
    pieces = []
    terms = jnp.zeros((2, input_count), jnp.float32)
    geom = jnp.zeros((input_count,), jnp.float32)
    for stripe in range(block_count):
        offset = tile_width * stripe * (stripe + 1) // 2
        start = stripe * tile_width
        span = (stripe + 1) * tile_width
        model_real = model[0, :, offset : offset + span].astype(jnp.float32)
        model_imag = model[1, :, offset : offset + span].astype(jnp.float32)
        row_real = gain_real[start:span][:, None]
        row_imag = gain_imag[start:span][:, None]
        outer_real = row_real * gain_real[None, :span] + row_imag * gain_imag[None, :span]
        outer_imag = row_imag * gain_real[None, :span] - row_real * gain_imag[None, :span]
        pred_real = outer_real * model_real - outer_imag * model_imag
        pred_imag = outer_real * model_imag + outer_imag * model_real
        gram_real, gram_imag = grams[stripe]
        res_real = gram_real * scale_factor - band_column * pred_real[None]
        res_imag = gram_imag * scale_factor - band_column * pred_imag[None]
        pieces.append(jnp.stack([res_real, res_imag], axis=1))
        q_real = (band_column * (res_real * model_real[None] + res_imag * model_imag[None])).astype(
            jnp.bfloat16
        )
        q_imag = (band_column * (res_imag * model_real[None] - res_real * model_imag[None])).astype(
            jnp.bfloat16
        )
        terms = terms + strip_terms(
            q_real, q_imag, short_real, short_imag, stripe, tile_width, input_count
        )
        weight_sq = model_real * model_real + model_imag * model_imag
        geom = geom.at[start:span].add(jnp.sum(weight_sq * power_gain[None, :span], axis=1))
        geom = geom.at[:span].add(jnp.sum(power_gain[start:span][:, None] * weight_sq, axis=0))
    residual = jnp.concatenate(pieces, axis=-1)
    grad_local = -terms
    band_power = jnp.sum(bandpass * bandpass)
    share_count = input_count // lax.axis_size("chan")
    first_input = lax.axis_index("chan") * share_count
    grad_whole, power = lax.psum((grad_local, band_power), "chan")
    updated = gains - 0.5 * grad_whole / (power * geom)[None, :]
    new_gains = lax.dynamic_slice_in_dim(updated, first_input, share_count, 1)
    return (residual, new_gains)


def solution(mesh):
    in_specs = (
        P("chan", "grp", None),
        P("chan", "grp", None),
        P(),
        P(None, "grp"),
        P(("grp", "chan")),
    )
    out_specs = (P(("grp", "chan"), None, None, None), P(None, ("grp", "chan")))
    return jax.shard_map(shards, mesh=mesh, in_specs=in_specs, out_specs=out_specs, check_vma=False)
```

profile of v0, /device:TPU:0, one launch (start us, length us, event | category | flops | bytes accessed | tf_op | source)
XLA Modules:
  0.0 158.1 jit_solution(16802452118391094419)
XLA Ops:
  0.6 2.7 %copy_convert_fusion = bf16[16,16,1024]{2,0,1:T(8,128)(2,1)} fusion(s32[16,16,1024]{2,1,0:T(8,128)} %param.108), kind=kLoop, calls=%fused_computation.207 | loop fusion | flops 262144 | bytes 1572864 | tf_op jit(solution)/shard_map/convert_element_type | solution.py:49
  3.3 7.4 %all-to-all-start.1 = ((bf16[16,16,1024]{2,0,1:T(8,128)(2,1)}), bf16[16,16,1024]{2,0,1:T(8,128)(2,1)S(1)}, u32[]{:S(2)}, u32[]{:S(2)}) async-start(bf16[16,16,1024]{2,0,1:T(8,128)(2,1)} %copy_convert_fusion), calls=%async_computation.1 | async-start | bytes 1048576 | tf_op jit(solution)/shard_map/all_to_all | solution.py:53
  21.5 1.4 copy_convert_fusion.1
  22.8 2.4 %all-to-all-done.1 = bf16[16,16,1024]{2,0,1:T(8,128)(2,1)S(1)} async-done(((bf16[16,16,1024]{2,0,1:T(8,128)(2,1)}), bf16[16,16,1024]{2,0,1:T(8,128)(2,1)S(1)}, u32[]{:S(2)}, u32[]{:S(2)}) %all-to-all-start.1) | async-done | bytes 524320 | tf_op jit(solution)/shard_map/all_to_all | solution.py:53
  25.2 4.1 %all-to-all-start = ((bf16[16,16,1024]{2,0,1:T(8,128)(2,1)}), bf16[16,16,1024]{2,0,1:T(8,128)(2,1)S(1)}, u32[]{:S(2)}, u32[]{:S(2)}) async-start(bf16[16,16,1024]{2,0,1:T(8,128)(2,1)} %copy_convert_fusion.1), calls=%async_computation | async-start | bytes 1048576 | tf_op jit(solution)/shard_map/all_to_all | solution.py:52
  30.5 13.2 %all-to-all-done = bf16[16,16,1024]{2,0,1:T(8,128)(2,1)S(1)} async-done(((bf16[16,16,1024]{2,0,1:T(8,128)(2,1)}), bf16[16,16,1024]{2,0,1:T(8,128)(2,1)S(1)}, u32[]{:S(2)}, u32[]{:S(2)}) %all-to-all-start) | async-done | bytes 524320 | tf_op jit(solution)/shard_map/all_to_all | solution.py:52
  43.8 1.6 %fusion = f32[128,1024]{1,0:T(8,128)S(1)} fusion(bf16[256,1,1024]{2,0,1:T(8,128)(2,1)S(1)} %bitcast.859, bf16[256,1,1024]{2,0,1:T(8,128)(2,1)S(1)} %bitcast.842, f32[1024]{0:T(1024)S(1)} %bitcast.906, f32[128]{0:T(128)S(1)} %get-tuple-element.666, f32[1024]{0:T(1024)S(1)} %bitcast.902, f32[128]{0:T(128)S(1)} %get-tuple-element.665, f32[]{:T(128)} %bitcast.832, ...), kind=kOutput, calls=%fused_computation.46 | convolution fusion | flops 138412032 | bytes 3154948 | tf_op jit(solution)/shard_map/scr,scn->crn/dot_general | solution.py:10
  45.6 2.1 %multiply_reduce_fusion = (f32[1024]{0:T(1024)}, f32[128]{0:T(128)}, bf16[128,1024]{1,0:T(8,128)(2,1)S(1)}, bf16[128,1024]{1,0:T(8,128)(2,1)S(1)}, f32[128,1024]{1,0:T(8,128)}) fusion(f32[128]{0:T(128)S(1)} %get-tuple-element.685, bf16[2,128,4608]{2,1,0:T(8,128)(2,1)S(1)} %copy-done.28, f32[1024]{0:T(1024)S(1)} %bitcast.938, f32[128,1024]{1,0:T(8,128)S(1)} %fusion, ...), kind=kOutput, calls=%fused_computation.280 | convolution fusion | flops 140639104 | bytes 4212740 | tf_op jit(solution)/shard_map/scr,scn->crn/dot_general | solution.py:10
  52.5 2.0 %multiply_reduce_fusion.2 = (f32[896]{0:T(1024)}, f32[128]{0:T(128)}, bf16[128,896]{1,0:T(8,128)(2,1)S(1)}, bf16[128,896]{1,0:T(8,128)(2,1)S(1)}, f32[128,896]{1,0:T(8,128)}) fusion(f32[128]{0:T(128)S(1)} %get-tuple-element.686, bf16[2,128,4608]{2,1,0:T(8,128)(2,1)S(1)} %copy-done.28, f32[896]{0:T(1024)S(1)} %bitcast.895, f32[128,896]{1,0:T(8,128)S(1)} %fusion.3, ...), kind=kOutput, calls=%fused_computation.295 | convolution fusion | flops 123091968 | bytes 3950084 | tf_op jit(solution)/shard_map/scr,scn->crn/dot_general | solution.py:10
  57.9 1.9 %multiply_reduce_fusion.4 = (f32[768]{0:T(1024)}, f32[128]{0:T(128)}, bf16[128,768]{1,0:T(8,128)(2,1)S(1)}, bf16[128,768]{1,0:T(8,128)(2,1)S(1)}, f32[128,768]{1,0:T(8,128)}) fusion(f32[128]{0:T(128)S(1)} %get-tuple-element.687, bf16[2,128,4608]{2,1,0:T(8,128)(2,1)S(1)} %copy-done.28, f32[768]{0:T(1024)S(1)} %bitcast.896, f32[128,768]{1,0:T(8,128)S(1)} %fusion.5, ...), kind=kOutput, calls=%fused_computation.325 | convolution fusion | flops 105544832 | bytes 3687428 | tf_op jit(solution)/shard_map/scr,scn->crn/dot_general | solution.py:10
  63.2 1.8 %multiply_reduce_fusion.6 = (f32[640]{0:T(1024)}, f32[128]{0:T(128)}, bf16[128,640]{1,0:T(8,128)(2,1)S(1)}, bf16[128,640]{1,0:T(8,128)(2,1)S(1)}, f32[128,640]{1,0:T(8,128)}) fusion(f32[128]{0:T(128)S(1)} %get-tuple-element.688, bf16[2,128,4608]{2,1,0:T(8,128)(2,1)S(1)} %copy-done.28, f32[640]{0:T(1024)S(1)} %bitcast.897, f32[128,640]{1,0:T(8,128)S(1)} %fusion.6, ...), kind=kOutput, calls=%fused_computation.340 | convolution fusion | flops 87997696 | bytes 3424772 | tf_op jit(solution)/shard_map/scr,scn->crn/dot_general | solution.py:10
  68.3 1.7 %multiply_reduce_fusion.8 = (f32[512]{0:T(512)}, f32[128]{0:T(128)}, bf16[128,512]{1,0:T(8,128)(2,1)S(1)}, bf16[128,512]{1,0:T(8,128)(2,1)S(1)}, f32[128,512]{1,0:T(8,128)}) fusion(f32[128]{0:T(128)S(1)} %get-tuple-element.689, bf16[2,128,4608]{2,1,0:T(8,128)(2,1)S(1)} %copy-done.28, f32[512]{0:T(512)S(1)} %slice.1148, f32[128,512]{1,0:T(8,128)S(1)} %fusion.8, ...), kind=kOutput, calls=%fused_computation.370 | convolution fusion | flops 70450560 | bytes 3155972 | tf_op jit(solution)/shard_map/scr,scn->crn/dot_general | solution.py:10
  73.1 1.6 multiply_reduce_fusion.10
  77.9 2.2 %multiply_reduce_fusion.12 = (f32[256]{0:T(256)}, f32[128]{0:T(128)}, bf16[128,256]{1,0:T(8,128)(2,1)S(1)}, bf16[128,256]{1,0:T(8,128)(2,1)S(1)}, f32[128,256]{1,0:T(8,128)}) fusion(f32[128]{0:T(128)S(1)} %copy-done.62, bf16[2,128,4608]{2,1,0:T(8,128)(2,1)S(1)} %copy-done.28, f32[256]{0:T(256)S(1)} %copy-done.59, f32[128,256]{1,0:T(8,128)S(1)} %fusion.13, ...), kind=kOutput, calls=%fused_computation.437 | convolution fusion | flops 35356288 | bytes 2627588 | tf_op jit(solution)/shard_map/scr,scn->crn/dot_general | solution.py:10
  83.2 1.4 multiply_reduce_fusion.14
  87.8 0.8 convolution_bitcast_fusion.13
  89.4 0.8 convolution_bitcast_fusion.15
  94.0 0.8 convolution_bitcast_fusion.4
  95.6 0.8 convolution_bitcast_fusion.6
  97.1 0.8 convolution_bitcast_fusion.33
  98.6 0.8 convolution_bitcast_fusion.35
  100.1 0.8 convolution_bitcast_fusion.8
  101.6 0.8 convolution_bitcast_fusion.10
  102.8 0.8 fusion.61
  103.6 0.9 fusion.65
  107.0 34.1 %all-reduce.15 = (f32[2,1024]{1,0:T(2,128)S(1)}, f32[]{:T(128)}) all-reduce(f32[2,1024]{1,0:T(2,128)S(1)} %fusion.242, f32[]{:T(128)} %bitcast.220), channel_id=1, replica_groups=mesh['grp'=2,'chan'=16] {'chan'}, use_global_device_ids=true, to_apply=%region_0.0 | all-reduce | flops 2049 | bytes 16392 | tf_op jit(solution)/shard_map/psum | solution.py:106
  151.6 1.8 %maximum_dynamic-update-slice_fusion.5 = f32[1,2,128,4608]{3,2,1,0:T(8,128)} fusion(f32[1,2,128,4608]{3,2,1,0:T(8,128)} %maximum_dynamic-update-slice_fusion.6, f32[1,1,128,384]{3,2,1,0:T(8,128)} %bitcast.894, f32[1,1,128,384]{3,2,1,0:T(8,128)S(1)} %bitcast.880), kind=kLoop, calls=%fused_computation.314 | loop fusion | flops 98304 | bytes 786432
  153.4 0.8 maximum_dynamic-update-slice_fusion.4
  154.2 0.9 maximum_dynamic-update-slice_fusion.3
  155.1 0.9 maximum_dynamic-update-slice_fusion.2
  156.1 1.0 maximum_dynamic-update-slice_fusion.1
  157.1 1.1 maximum_dynamic-update-slice_fusion
  (286 shorter events, 59.9 us)
Async XLA Ops:
  0.6 20.8 %copy-start.2 = (s32[16,16,1024]{2,1,0:T(8,128)S(1)}, s32[16,16,1024]{2,1,0:T(8,128)}, u32[]{:S(2)}) copy-start(s32[16,16,1024]{2,1,0:T(8,128)} %param.107) | copy-start | bytes 3145732
  3.3 21.9 %all-to-all-start.1 = ((bf16[16,16,1024]{2,0,1:T(8,128)(2,1)}), bf16[16,16,1024]{2,0,1:T(8,128)(2,1)S(1)}, u32[]{:S(2)}, u32[]{:S(2)}) async-start(bf16[16,16,1024]{2,0,1:T(8,128)(2,1)} %copy_convert_fusion), calls=%async_computation.1 | async-start | bytes 1048576 | tf_op jit(solution)/shard_map/all_to_all | solution.py:53
  21.4 56.1 %copy-start.51 = (f32[1,256]{1,0:T(1,128)}, f32[1,256]{1,0:T(1,128)S(1)}, u32[]{:S(2)}) copy-start(f32[1,256]{1,0:T(1,128)S(1)} %get-tuple-element.683) | copy-start | bytes 3076
  21.5 56.1 %copy-start.52 = (f32[1,256]{1,0:T(1,128)}, f32[1,256]{1,0:T(1,128)S(1)}, u32[]{:S(2)}) copy-start(f32[1,256]{1,0:T(1,128)S(1)} %get-tuple-element.684) | copy-start | bytes 3076
  25.2 18.6 %all-to-all-start = ((bf16[16,16,1024]{2,0,1:T(8,128)(2,1)}), bf16[16,16,1024]{2,0,1:T(8,128)(2,1)S(1)}, u32[]{:S(2)}, u32[]{:S(2)}) async-start(bf16[16,16,1024]{2,0,1:T(8,128)(2,1)} %copy_convert_fusion.1), calls=%async_computation | async-start | bytes 1048576 | tf_op jit(solution)/shard_map/all_to_all | solution.py:52
  30.5 47.0 %copy-start.56 = (f32[128]{0:T(128)}, f32[128]{0:T(128)S(1)}, u32[]{:S(2)}) copy-start(f32[128]{0:T(128)S(1)} %get-tuple-element.677) | copy-start | bytes 1540
  30.5 47.0 %copy-start.57 = (f32[128]{0:T(128)}, f32[128]{0:T(128)S(1)}, u32[]{:S(2)}) copy-start(f32[128]{0:T(128)S(1)} %get-tuple-element.678) | copy-start | bytes 1540
  84.7 19.8 %copy-start.32 = (bf16[896,1]{0,1:T(2,128)(2,1)S(1)}, bf16[896,1]{0,1:T(2,128)(2,1)}, u32[]{:S(2)}) copy-start(bf16[896,1]{0,1:T(2,128)(2,1)} %reshape.1559) | copy-start | bytes 5380
  84.7 20.0 %copy-start.30 = (bf16[896,1]{0,1:T(2,128)(2,1)S(1)}, bf16[896,1]{0,1:T(2,128)(2,1)}, u32[]{:S(2)}) copy-start(bf16[896,1]{0,1:T(2,128)(2,1)} %reshape.1557) | copy-start | bytes 5380
  84.7 20.2 %copy-start.34 = (bf16[768,1]{0,1:T(2,128)(2,1)S(1)}, bf16[768,1]{0,1:T(2,128)(2,1)}, u32[]{:S(2)}) copy-start(bf16[768,1]{0,1:T(2,128)(2,1)} %reshape.1541) | copy-start | bytes 4612
  84.7 20.4 %copy-start.33 = (bf16[768,1]{0,1:T(2,128)(2,1)S(1)}, bf16[768,1]{0,1:T(2,128)(2,1)}, u32[]{:S(2)}) copy-start(bf16[768,1]{0,1:T(2,128)(2,1)} %reshape.1543) | copy-start | bytes 4612
  84.7 20.5 %copy-start.36 = (bf16[640,1]{0,1:T(2,128)(2,1)S(1)}, bf16[640,1]{0,1:T(2,128)(2,1)}, u32[]{:S(2)}) copy-start(bf16[640,1]{0,1:T(2,128)(2,1)} %reshape.1525) | copy-start | bytes 3844
  84.7 20.7 %copy-start.35 = (bf16[640,1]{0,1:T(2,128)(2,1)S(1)}, bf16[640,1]{0,1:T(2,128)(2,1)}, u32[]{:S(2)}) copy-start(bf16[640,1]{0,1:T(2,128)(2,1)} %reshape.1527) | copy-start | bytes 3844
  86.4 19.4 %copy-start.37 = (bf16[512,1]{0,1:T(2,128)(2,1)S(1)}, bf16[512,1]{0,1:T(2,128)(2,1)}, u32[]{:S(2)}) copy-start(bf16[512,1]{0,1:T(2,128)(2,1)} %reshape.1509) | copy-start | bytes 3076
  86.4 19.6 %copy-start.50 = (bf16[384,1]{0,1:T(2,128)(2,1)S(1)}, bf16[384,1]{0,1:T(2,128)(2,1)}, u32[]{:S(2)}) copy-start(bf16[384,1]{0,1:T(2,128)(2,1)} %reshape.1493) | copy-start | bytes 2308
  86.5 19.6 %copy-start.49 = (bf16[384,1]{0,1:T(2,128)(2,1)S(1)}, bf16[384,1]{0,1:T(2,128)(2,1)}, u32[]{:S(2)}) copy-start(bf16[384,1]{0,1:T(2,128)(2,1)} %reshape.1495) | copy-start | bytes 2308
  86.5 19.8 %copy-start.7 = (bf16[128,256]{1,0:T(8,128)(2,1)S(1)}, bf16[128,256]{1,0:T(8,128)(2,1)}, u32[]{:S(2)}) copy-start(bf16[128,256]{1,0:T(8,128)(2,1)} %copy-done.6) | copy-start | bytes 196612
  86.5 19.8 %copy-start.64 = (bf16[256,1]{0,1:T(2,128)(2,1)S(1)}, bf16[256,1]{0,1:T(2,128)(2,1)}, u32[]{:S(2)}) copy-start(bf16[256,1]{0,1:T(2,128)(2,1)} %reshape.1479) | copy-start | bytes 1540
  86.5 19.9 %copy-start.63 = (bf16[256,1]{0,1:T(2,128)(2,1)S(1)}, bf16[256,1]{0,1:T(2,128)(2,1)}, u32[]{:S(2)}) copy-start(bf16[256,1]{0,1:T(2,128)(2,1)} %reshape.1477) | copy-start | bytes 1540
  86.6 20.1 %copy-start.22 = (bf16[128,128]{0,1:T(8,128)(2,1)S(1)}, bf16[128,128]{0,1:T(8,128)(2,1)}, u32[]{:S(2)}) copy-start(bf16[128,128]{0,1:T(8,128)(2,1)} %get-tuple-element.661) | copy-start | bytes 98308
  87.2 19.5 %copy-start.65 = (f32[128]{0:T(128)S(1)}, f32[128]{0:T(128)}, u32[]{:S(2)}) copy-start(f32[128]{0:T(128)} %convolution_bitcast_fusion.21) | copy-start | bytes 1540
  87.3 55.1 %copy-start.58 = (f32[256]{0:T(256)S(1)}, f32[256]{0:T(256)}, u32[]{:S(2)}) copy-start(f32[256]{0:T(256)} %get-tuple-element.614) | copy-start | bytes 3076
  87.3 62.3 %copy-start.60 = (f32[1024]{0:T(1024)S(1)}, f32[1024]{0:T(1024)}, u32[]{:S(2)}) copy-start(f32[1024]{0:T(1024)} %get-tuple-element.602) | copy-start | bytes 12292
  87.3 63.5 %copy-start.1 = (f32[128,256]{1,0:T(8,128)S(1)}, f32[128,256]{1,0:T(8,128)}, u32[]{:S(2)}) copy-start(f32[128,256]{1,0:T(8,128)} %copy-done) | copy-start | bytes 393220
  87.3 63.5 %copy-start.8 = (f32[128,256]{1,0:T(8,128)S(1)}, f32[128,256]{1,0:T(8,128)}, u32[]{:S(2)}) copy-start(f32[128,256]{1,0:T(8,128)} %get-tuple-element.699) | copy-start | bytes 393220
  87.8 63.8 %copy-start.4 = (f32[128,384]{1,0:T(8,128)S(1)}, f32[128,384]{1,0:T(8,128)}, u32[]{:S(2)}) copy-start(f32[128,384]{1,0:T(8,128)} %copy-done.3) | copy-start | bytes 589828
  94.9 58.5 %copy-start.24 = (f32[128,512]{1,0:T(8,128)S(1)}, f32[128,512]{1,0:T(8,128)}, u32[]{:S(2)}) copy-start(f32[128,512]{1,0:T(8,128)} %copy-done.23) | copy-start | bytes 786436
  94.9 58.5 %copy-start.25 = (f32[128,512]{1,0:T(8,128)S(1)}, f32[128,512]{1,0:T(8,128)}, u32[]{:S(2)}) copy-start(f32[128,512]{1,0:T(8,128)} %get-tuple-element.697) | copy-start | bytes 786436
  103.6 50.6 %copy-start.19 = (f32[128,640]{1,0:T(8,128)S(1)}, f32[128,640]{1,0:T(8,128)}, u32[]{:S(2)}) copy-start(f32[128,640]{1,0:T(8,128)} %copy-done.18) | copy-start | bytes 983044
  103.6 50.6 %copy-start.20 = (f32[128,640]{1,0:T(8,128)S(1)}, f32[128,640]{1,0:T(8,128)}, u32[]{:S(2)}) copy-start(f32[128,640]{1,0:T(8,128)} %get-tuple-element.696) | copy-start | bytes 983044
  105.4 49.7 %copy-start.16 = (f32[128,768]{1,0:T(8,128)S(1)}, f32[128,768]{1,0:T(8,128)}, u32[]{:S(2)}) copy-start(f32[128,768]{1,0:T(8,128)} %copy-done.15) | copy-start | bytes 1179652
  105.4 49.7 %copy-start.17 = (f32[128,768]{1,0:T(8,128)S(1)}, f32[128,768]{1,0:T(8,128)}, u32[]{:S(2)}) copy-start(f32[128,768]{1,0:T(8,128)} %get-tuple-element.695) | copy-start | bytes 1179652
  (37 other events, 258.4 us)
where the time goes:
time: 159 us; the launch traced here: 158 us
  matrix products  54.6 us (34%)
  blocking collectives  34.1 us (21%)
  other arithmetic  27.7 us (17%)
  waiting for transfers between devices  15.6 us (10%)
  local copies, waits for them, and re-layouts  12.5 us (8%)
  starting transfers between devices  11.5 us (7%)
  between operations  2.15 us (1%)
    psum x1, blocking collectives, shards(): grad_whole, power = lax.psum((grad_local, band_power), 'chan')  34.1 us
    dot_general x16, matrix products, strip_product(): jnp.einsum('scr,scn->crn', row_part, col_part, preferred_element_type=jnp...  18.5 us
    all_to_all x1, waiting for transfers between devices, shards(): lax.all_to_all(real_send, 'chan', split_axis=1, concat_axis=0, tiled=True)  13.2 us
    all_to_all x1, starting transfers between devices, shards(): lax.all_to_all(imag_send, 'chan', split_axis=1, concat_axis=0, tiled=True)  7.39 us
    unnamed x6, other arithmetic  6.13 us
    dot_general x8, matrix products, strip_terms(): jnp.einsum('r,crn->n', own_imag, q_real, preferred_element_type=f32)  5.26 us
    dot_general x8, matrix products, strip_terms(): jnp.einsum('r,crn->n', own_real, q_imag, preferred_element_type=f32)  5.26 us
    dot_general x8, matrix products, strip_terms(): jnp.einsum('r,crn->n', own_real, q_real, preferred_element_type=f32)  5.23 us
  transfers between devices with their start and end apart: 2, of which 2 were waited for; matrix products, arithmetic and copies ran while one was open for 8% of the time, Pallas kernels for 0%

commit v1 on v0

v1 whole, which is shorter than its diff:
```python
import functools

import jax
import jax.numpy as jnp
from jax import lax
from jax.experimental import pallas as pl
from jax.experimental.pallas import tpu as pltpu
from jax.sharding import PartitionSpec as P

F32 = jnp.float32
BF16 = jnp.bfloat16
LANES = 128


def partner_of(me, step, count):
    total = 0
    bit = 1
    while bit < count:
        total = total + lax.rem(lax.div(me, bit) + lax.div(step, bit), 2) * bit
        bit *= 2
    return total


def lane_block(index):
    return pl.ds(pl.multiple_of(index * LANES, LANES), LANES)


def fold_rows(block):
    return jnp.sum(block.reshape(block.shape[0] // 8, 8, block.shape[1]), axis=0)


def column_sum(block):
    return jnp.sum(block, axis=0, keepdims=True)


def kernel(
    count,
    scale,
    vr_hbm,
    vi_hbm,
    model_hbm,
    gain_ref,
    band_ref,
    res_ref,
    new_ref,
    ints,
    outgoing,
    volts,
    swapped,
    model,
    gain_rows,
    row_acc,
    col_acc,
    geom_col,
    geom_all,
    terms,
    incoming,
    load_sem,
    model_sem,
    send_sem,
    recv_sem,
    term_send,
    term_recv,
):
    me = lax.axis_index("chan")
    inputs = gain_ref.shape[1]
    blocks = inputs // LANES
    samples = ints.shape[2] // count
    share = new_ref.shape[1]

    loads = []
    for which, source in enumerate((vr_hbm, vi_hbm)):
        for lane in range(blocks):
            load = pltpu.make_async_copy(
                source.at[:, lane * LANES : (lane + 1) * LANES],
                ints.at[which, lane],
                load_sem.at[which, lane],
            )
            load.start()
            loads.append(load)
    load_model = pltpu.make_async_copy(model_hbm, model, model_sem)

    barrier = pltpu.get_barrier_semaphore()

    @pl.loop(1, count)
    def _(step):
        pl.semaphore_signal(
            barrier,
            inc=1,
            device_id={"chan": partner_of(me, step, count)},
            device_id_type=pl.DeviceIdType.MESH,
        )

    for load in loads:
        load.wait()
    load_model.start()
    pl.semaphore_wait(barrier, count - 1)

    def volt_copy(step):
        return pltpu.make_async_remote_copy(
            src_ref=outgoing.at[step],
            dst_ref=volts.at[step],
            send_sem=send_sem.at[step],
            recv_sem=recv_sem.at[step],
            device_id={"chan": partner_of(me, step, count)},
            device_id_type=pl.DeviceIdType.MESH,
        )

    def short_rows(which, channel, lane):
        rows = ints[which, lane, pl.ds(channel, samples, stride=count), :]
        return rows.astype(F32).astype(BF16)

    @pl.loop(0, count - 1)
    def _(turn):
        step = count - 1 - turn
        channel = partner_of(me, step, count)
        for lane in range(blocks):
            cols = slice(lane * LANES, (lane + 1) * LANES)
            outgoing[step, 0:samples, cols] = short_rows(0, channel, lane)
            outgoing[step, samples : 2 * samples, cols] = short_rows(1, channel, lane)
        volt_copy(step).start()

    for lane in range(blocks):
        cols = slice(lane * LANES, (lane + 1) * LANES)
        volts[0, 0:samples, cols] = short_rows(0, me, lane)
        volts[0, samples : 2 * samples, cols] = short_rows(1, me, lane)

    band = band_ref[0]

    @pl.loop(0, blocks)
    def _(p):
        for part in range(2):
            line = gain_ref[part : part + 1, lane_block(p)]
            gain_rows[part, lane_block(p), :] = jnp.broadcast_to(line, (LANES, LANES)).T
        geom_col[p] = jnp.zeros((8, LANES), F32)
        col_acc[p] = jnp.zeros((2, 8, LANES), F32)

    load_model.wait()

    @pl.loop(0, blocks)
    def _(p):
        row_acc[0] = jnp.zeros((LANES, LANES), F32)
        rows = lane_block(p)

        @pl.loop(0, p + 1)
        def _(j):
            place = lane_block(lax.div(p * (p + 1), 2) + j)
            model_real = model[0, :, place].astype(F32)
            model_imag = model[1, :, place].astype(F32)
            row_real = gain_rows[0, rows, :]
            row_imag = gain_rows[1, rows, :]
            col_real = gain_ref[0:1, lane_block(j)]
            col_imag = gain_ref[1:2, lane_block(j)]
            outer_real = row_real * col_real + row_imag * col_imag
            outer_imag = row_imag * col_real - row_real * col_imag
            res_ref[0, 0, :, place] = -band * (outer_real * model_real - outer_imag * model_imag)
            res_ref[0, 1, :, place] = -band * (outer_real * model_imag + outer_imag * model_real)
            weight_sq = model_real * model_real + model_imag * model_imag
            row_acc[0] += weight_sq * (col_real * col_real + col_imag * col_imag)
            geom_col[j] += fold_rows((row_real * row_real + row_imag * row_imag) * weight_sq)

        geom_all[p] = column_sum(row_acc[0].T)

    def gather_products(first, last):
        @pl.loop(max(first, 1), last)
        def _(step):
            volt_copy(step).wait_recv()

        @pl.loop(first, last)
        def _(step):
            swapped[step, 0:samples, :] = -volts[step, samples : 2 * samples, :]
            swapped[step, samples : 2 * samples, :] = volts[step, 0:samples, :]

        depth = (last - first) * 2 * samples
        wide = 2 * LANES
        for pair in range(blocks // 2):
            left = volts[first:last, :, pair * wide : (pair + 1) * wide].reshape(depth, wide)
            for tile in range(pair + 1):
                for part, source in ((0, volts), (1, swapped)):
                    right = source[first:last, :, tile * wide : (tile + 1) * wide].reshape(depth, wide)
                    product = scale * lax.dot_general(
                        left, right, (((0,), (0,)), ((), ())), preferred_element_type=F32
                    )
                    for half in range(2):
                        stripe = 2 * pair + half
                        offset = stripe * (stripe + 1) // 2 * LANES + tile * wide
                        width = min(wide, (stripe + 1) * LANES - tile * wide)
                        res_ref[0, part, :, offset : offset + width] += product[
                            half * LANES : (half + 1) * LANES, :width
                        ]

    gather_products(0, count // 2)
    gather_products(count // 2, count)

    @pl.loop(0, blocks)
    def _(p):
        row_acc[...] = jnp.zeros((2, LANES, LANES), F32)
        rows = lane_block(p)

        @pl.loop(0, p + 1)
        def _(j):
            place = lane_block(lax.div(p * (p + 1), 2) + j)
            model_real = model[0, :, place].astype(F32)
            model_imag = model[1, :, place].astype(F32)
            res_real = res_ref[0, 0, :, place]
            res_imag = res_ref[0, 1, :, place]
            q_real = (band * (res_real * model_real + res_imag * model_imag)).astype(BF16).astype(F32)
            q_imag = (band * (res_imag * model_real - res_real * model_imag)).astype(BF16).astype(F32)
            col_real = gain_ref[0:1, lane_block(j)].astype(BF16).astype(F32)
            col_imag = gain_ref[1:2, lane_block(j)].astype(BF16).astype(F32)
            row_real = gain_rows[0, rows, :].astype(BF16).astype(F32)
            row_imag = gain_rows[1, rows, :].astype(BF16).astype(F32)
            row_acc[0] += q_real * col_real - q_imag * col_imag
            row_acc[1] += q_real * col_imag + q_imag * col_real
            col_acc[j, 0] += fold_rows(row_real * q_real + row_imag * q_imag)
            col_acc[j, 1] += fold_rows(row_imag * q_real - row_real * q_imag)

        terms[p, 0:1] = column_sum(row_acc[0].T)
        terms[p, 1:2] = column_sum(row_acc[1].T)
        terms[p, 2:3] = jnp.full((1, LANES), band * band, F32)
        terms[p, 3:8] = jnp.zeros((5, LANES), F32)

    @pl.loop(0, blocks)
    def _(p):
        terms[p, 0:1] += column_sum(col_acc[p, 0])
        terms[p, 1:2] += column_sum(col_acc[p, 1])

    def term_copy(step):
        target = partner_of(me, step, count)
        return pltpu.make_async_remote_copy(
            src_ref=terms.at[lax.div(target * share, LANES)],
            dst_ref=incoming.at[step],
            send_sem=term_send.at[step],
            recv_sem=term_recv.at[step],
            device_id={"chan": target},
            device_id_type=pl.DeviceIdType.MESH,
        )

    @pl.loop(0, count - 1)
    def _(turn):
        term_copy(count - 1 - turn).start()

    mine = lax.div(me * share, LANES)
    incoming[0] = terms[mine]

    @pl.loop(1, count)
    def _(step):
        volt_copy(step).wait_send()
        term_copy(step).wait()

    total = jnp.sum(incoming[...], axis=0)
    geom = geom_all[mine] + column_sum(geom_col[mine])
    updated = gain_ref[:, lane_block(mine)] + 0.5 * total[0:2] / (total[2:3] * geom)
    lane_group = lax.rem(me, LANES // share)
    picked = updated[:, 0:share]
    for group in range(1, LANES // share):
        picked = jnp.where(lane_group == group, updated[:, group * share : (group + 1) * share], picked)
    new_ref[...] = picked


def shards(voltages_real, voltages_imag, model, gains, bandpass):
    count = lax.axis_size("chan")
    samples, channels, inputs = voltages_real.shape
    scale = 1.0 / (4096.0 * samples * count)
    blocks = inputs // LANES
    share = inputs // count
    anywhere = pl.BlockSpec(memory_space=pl.ANY)
    in_vmem = pl.BlockSpec(memory_space=pltpu.VMEM)
    return pl.pallas_call(
        functools.partial(kernel, count, scale),
        out_shape=(
            jax.ShapeDtypeStruct((1,) + model.shape, F32),
            jax.ShapeDtypeStruct((2, share), F32),
        ),
        in_specs=[anywhere, anywhere, anywhere, in_vmem, pl.BlockSpec(memory_space=pltpu.SMEM)],
        out_specs=(in_vmem, in_vmem),
        scratch_shapes=[
            pltpu.VMEM((2, blocks, samples * channels, LANES), jnp.int32),
            pltpu.VMEM((count, 2 * samples, inputs), BF16),
            pltpu.VMEM((count, 2 * samples, inputs), BF16),
            pltpu.VMEM((count, 2 * samples, inputs), BF16),
            pltpu.VMEM(model.shape, BF16),
            pltpu.VMEM((2, inputs, LANES), F32),
            pltpu.VMEM((2, LANES, LANES), F32),
            pltpu.VMEM((blocks, 2, 8, LANES), F32),
            pltpu.VMEM((blocks, 8, LANES), F32),
            pltpu.VMEM((blocks, 1, LANES), F32),
            pltpu.VMEM((blocks, 8, LANES), F32),
            pltpu.VMEM((count, 8, LANES), F32),
            pltpu.SemaphoreType.DMA((2, blocks)),
            pltpu.SemaphoreType.DMA,
            pltpu.SemaphoreType.DMA((count,)),
            pltpu.SemaphoreType.DMA((count,)),
            pltpu.SemaphoreType.DMA((count,)),
            pltpu.SemaphoreType.DMA((count,)),
        ],
        compiler_params=pltpu.CompilerParams(
            collective_id=0, has_side_effects=True, vmem_limit_bytes=50 * 1024 * 1024
        ),
        cost_estimate=pl.CostEstimate(
            flops=4 * samples * count * inputs * inputs, bytes_accessed=10 * 1024 * 1024, transcendentals=0
        ),
    )(
        voltages_real.reshape(samples * channels, inputs),
        voltages_imag.reshape(samples * channels, inputs),
        model,
        gains,
        bandpass,
    )


def solution(mesh):
    in_specs = (
        P("chan", "grp", None),
        P("chan", "grp", None),
        P(),
        P(None, "grp"),
        P(("grp", "chan")),
    )
    out_specs = (P(("grp", "chan"), None, None, None), P(None, ("grp", "chan")))
    return jax.shard_map(shards, mesh=mesh, in_specs=in_specs, out_specs=out_specs, check_vma=False)
```

time: 159 us -> 52.9 us (0.33)
  matrix products: 54.6 us -> 0 us
  Pallas kernels: 0 us -> 42.8 us
  blocking collectives: 34.1 us -> 0 us
  other arithmetic: 27.7 us -> 0 us
  waiting for transfers between devices: 15.6 us -> 0 us
  starting transfers between devices: 11.5 us -> 0 us
  local copies, waits for them, and re-layouts: 12.5 us -> 8.54 us
    dot_general x80 -> x0, matrix products: 54.6 us -> none  [the longest x16 18.5 us: strip_product(): jnp.einsum('scr,scn->crn', row_part, col_part, preferred_element_type=jnp...]
    pallas_call x0 -> x1, Pallas kernels: none -> 42.8 us  [shards(): pl.pallas_call(functools.partial(kernel, count, scale), out_shape=(jax.Sh...]
    psum x1 -> x0, blocking collectives: 34.1 us -> none  [shards(): grad_whole, power = lax.psum((grad_local, band_power), 'chan')]
    all_to_all x2 -> x0, waiting for transfers between devices: 15.6 us -> none  [the longest x1 13.2 us: shards(): lax.all_to_all(real_send, 'chan', split_axis=1, concat_axis=0, tiled=True)]
    all_to_all x2 -> x0, starting transfers between devices: 11.5 us -> none  [the longest x1 7.39 us: shards(): lax.all_to_all(imag_send, 'chan', split_axis=1, concat_axis=0, tiled=True)]
    slice x29 -> x0, local copies, waits for them, and re-layouts: 9.15 us -> none  [the longest x9 3.55 us: strip_terms(): col_real = gain_real[:span]]
    scatter-add x14 -> x0, other arithmetic: 8.48 us -> none  [the longest x7 4.39 us: shards(): geom.at[start:span]]
    unnamed x6 -> x0, other arithmetic: 6.13 us -> none
  transfers between devices with their start and end apart: 2 -> 0, of which waited for: 2 -> 0; matrix products, arithmetic and copies ran while one was open for 8% -> 0% of each run, Pallas kernels for 0% -> 0%
where the time goes in v1:
time: 52.9 us; the launch traced here: 52.6 us
  Pallas kernels  42.8 us (81%)
  local copies, waits for them, and re-layouts  8.54 us (16%)
  between operations  1.3 us (2%)
    pallas_call x1, Pallas kernels, shards(): pl.pallas_call(functools.partial(kernel, count, scale), out_shape=(jax.Sh...  42.8 us
    unnamed x8, local copies, waits for them, and re-layouts  8.54 us

profile of v1, /device:TPU:0, one launch (start us, length us, event | category | flops | bytes accessed | tf_op | source)
XLA Modules:
  0.0 52.6 jit_solution(4099361808157312773)
XLA Ops:
  1.3 0.0 copy-start
  1.3 1.2 %copy-done = s32[16,16,1024]{2,1,0:T(8,128)S(1)} copy-done((s32[16,16,1024]{2,1,0:T(8,128)S(1)}, s32[16,16,1024]{2,1,0:T(8,128)}, u32[]{:S(2)}) %copy-start) | copy-done | bytes 1048600
  2.5 0.0 copy-start.1
  2.5 1.2 %copy-done.1 = s32[16,16,1024]{2,1,0:T(8,128)S(1)} copy-done((s32[16,16,1024]{2,1,0:T(8,128)S(1)}, s32[16,16,1024]{2,1,0:T(8,128)}, u32[]{:S(2)}) %copy-start.1) | copy-done | bytes 1048600
  3.7 0.0 copy-start.2
  3.7 0.7 %copy-done.2 = f32[2,1024]{1,0:T(2,128)S(1)} copy-done((f32[2,1024]{1,0:T(2,128)S(1)}, f32[2,1024]{1,0:T(2,128)}, u32[]{:S(2)}) %copy-start.2) | copy-done | bytes 8216
  4.4 42.8 %shard_map.68 = (f32[1,2,128,4608]{3,2,1,0:T(8,128)}, f32[2,64]{1,0:T(2,128)S(1)}) custom-call(s32[256,1024]{1,0:T(8,128)S(1)} %bitcast.2, s32[256,1024]{1,0:T(8,128)S(1)} %bitcast.3, bf16[2,128,4608]{2,1,0:T(8,128)(2,1)} %model_hbm.1, f32[2,1024]{1,0:T(2,128)S(1)} %copy-done.2, f32[1]{0:T(128)S(6)} %copy.9.band_ref), custom_call_target="tpu_custom_call" | custom-call | flops 1073741824 | bytes 10485760 | tf_op jit(solution)/shard_map/pallas_call | solution.py:269
  47.2 4.8 %copy.10 = f32[1,2,128,4608]{3,2,1,0:T(8,128)} copy(f32[1,2,128,4608]{3,2,1,0:T(8,128)} %get-tuple-element.4) | data formatting | bytes 9437184
  52.1 0.6 %copy.11 = f32[2,64]{1,0:T(2,128)} copy(f32[2,64]{1,0:T(2,128)S(1)} %get-tuple-element.5) | data formatting | bytes 1024
Async XLA Ops:
  1.3 1.2 %copy-start = (s32[16,16,1024]{2,1,0:T(8,128)S(1)}, s32[16,16,1024]{2,1,0:T(8,128)}, u32[]{:S(2)}) copy-start(s32[16,16,1024]{2,1,0:T(8,128)} %param.5) | copy-start | bytes 3145732
  2.5 1.2 %copy-start.1 = (s32[16,16,1024]{2,1,0:T(8,128)S(1)}, s32[16,16,1024]{2,1,0:T(8,128)}, u32[]{:S(2)}) copy-start(s32[16,16,1024]{2,1,0:T(8,128)} %param.6) | copy-start | bytes 3145732
  3.7 0.7 %copy-start.2 = (f32[2,1024]{1,0:T(2,128)S(1)}, f32[2,1024]{1,0:T(2,128)}, u32[]{:S(2)}) copy-start(f32[2,1024]{1,0:T(2,128)} %gain_ref.1) | copy-start | bytes 24580

commit v2 on v1

--- a/solution.py
+++ b/solution.py
@@ -39,7 +39,7 @@
     vr_hbm,
     vi_hbm,
     model_hbm,
-    gain_ref,
+    gain_hbm,
     band_ref,
     res_ref,
     new_ref,
@@ -48,6 +48,7 @@
     volts,
     swapped,
     model,
+    gain_ref,
     gain_rows,
     row_acc,
     col_acc,
@@ -57,6 +58,7 @@
     incoming,
     load_sem,
     model_sem,
+    gain_sem,
     send_sem,
     recv_sem,
     term_send,
@@ -78,6 +80,7 @@
             )
             load.start()
             loads.append(load)
+    load_gains = pltpu.make_async_copy(gain_hbm, gain_ref, gain_sem)
     load_model = pltpu.make_async_copy(model_hbm, model, model_sem)
 
     barrier = pltpu.get_barrier_semaphore()
@@ -93,6 +96,7 @@
 
     for load in loads:
         load.wait()
+    load_gains.start()
     load_model.start()
     pl.semaphore_wait(barrier, count - 1)
 
@@ -126,6 +130,7 @@
         volts[0, samples : 2 * samples, cols] = short_rows(1, me, lane)
 
     band = band_ref[0]
+    load_gains.wait()
 
     @pl.loop(0, blocks)
     def _(p):
@@ -264,15 +269,15 @@
     scale = 1.0 / (4096.0 * samples * count)
     blocks = inputs // LANES
     share = inputs // count
-    anywhere = pl.BlockSpec(memory_space=pl.ANY)
+    in_hbm = pl.BlockSpec(memory_space=pltpu.HBM)
     in_vmem = pl.BlockSpec(memory_space=pltpu.VMEM)
     return pl.pallas_call(
         functools.partial(kernel, count, scale),
         out_shape=(
-            jax.ShapeDtypeStruct((1,) + model.shape, F32),
+            pltpu.VMEM((1,) + model.shape, F32),
             jax.ShapeDtypeStruct((2, share), F32),
         ),
-        in_specs=[anywhere, anywhere, anywhere, in_vmem, pl.BlockSpec(memory_space=pltpu.SMEM)],
+        in_specs=[in_hbm, in_hbm, in_hbm, in_hbm, pl.BlockSpec(memory_space=pltpu.SMEM)],
         out_specs=(in_vmem, in_vmem),
         scratch_shapes=[
             pltpu.VMEM((2, blocks, samples * channels, LANES), jnp.int32),
@@ -280,6 +285,7 @@
             pltpu.VMEM((count, 2 * samples, inputs), BF16),
             pltpu.VMEM((count, 2 * samples, inputs), BF16),
             pltpu.VMEM(model.shape, BF16),
+            pltpu.VMEM(gains.shape, F32),
             pltpu.VMEM((2, inputs, LANES), F32),
             pltpu.VMEM((2, LANES, LANES), F32),
             pltpu.VMEM((blocks, 2, 8, LANES), F32),
@@ -289,13 +295,14 @@
             pltpu.VMEM((count, 8, LANES), F32),
             pltpu.SemaphoreType.DMA((2, blocks)),
             pltpu.SemaphoreType.DMA,
+            pltpu.SemaphoreType.DMA,
             pltpu.SemaphoreType.DMA((count,)),
             pltpu.SemaphoreType.DMA((count,)),
             pltpu.SemaphoreType.DMA((count,)),
             pltpu.SemaphoreType.DMA((count,)),
         ],
         compiler_params=pltpu.CompilerParams(
-            collective_id=0, has_side_effects=True, vmem_limit_bytes=50 * 1024 * 1024
+            collective_id=0, has_side_effects=True, vmem_limit_bytes=52 * 1024 * 1024
         ),
         cost_estimate=pl.CostEstimate(
             flops=4 * samples * count * inputs * inputs, bytes_accessed=10 * 1024 * 1024, transcendentals=0

time: 52.9 us -> 45.4 us (0.86)
  local copies, waits for them, and re-layouts: 8.54 us -> 2.75 us
  Pallas kernels: 42.8 us -> 41.2 us
    unnamed x8 -> x4, local copies, waits for them, and re-layouts: 8.54 us -> 2.75 us
    pallas_call x1, Pallas kernels: 42.8 us -> 41.2 us  [shards(): pl.pallas_call(functools.partial(kernel, count, scale), out_shape=(pltpu....]
where the time goes in v2:
time: 45.4 us; the launch traced here: 45.3 us
  Pallas kernels  41.2 us (91%)
  local copies, waits for them, and re-layouts  2.75 us (6%)
  between operations  1.29 us (3%)
    pallas_call x1, Pallas kernels, shards(): pl.pallas_call(functools.partial(kernel, count, scale), out_shape=(pltpu....  41.2 us
    unnamed x4, local copies, waits for them, and re-layouts  2.75 us

profile of v2, /device:TPU:0, one launch (start us, length us, event | category | flops | bytes accessed | tf_op | source)
XLA Modules:
  0.0 45.3 jit_solution(7267487630626580502)
XLA Ops:
  1.3 41.2 %shard_map.68 = (f32[1,2,128,4608]{3,2,1,0:T(8,128)S(1)}, f32[2,64]{1,0:T(2,128)}) custom-call(s32[256,1024]{1,0:T(8,128)} %bitcast.2, s32[256,1024]{1,0:T(8,128)} %bitcast.3, bf16[2,128,4608]{2,1,0:T(8,128)(2,1)} %model_hbm.1, f32[2,1024]{1,0:T(2,128)} %gain_hbm.1, f32[1]{0:T(128)S(6)} %copy.10.band_ref), custom_call_target="tpu_custom_call" | custom-call | flops 1073741824 | bytes 10485760 | tf_op jit(solution)/shard_map/pallas_call | solution.py:274
  42.5 0.0 copy-start
  42.5 2.2 %copy.9 = f32[1,2,128,4608]{3,2,1,0:T(8,128)} copy(f32[1,2,128,4608]{3,2,1,0:T(8,128)S(1)} %get-tuple-element.2) | data formatting | bytes 9437184
  44.7 0.0 copy-done
  44.7 0.6 %copy.11 = f32[2,64]{1,0:T(2,128)} copy(f32[2,64]{1,0:T(2,128)S(1)} %copy-done) | data formatting | bytes 1024
Async XLA Ops:
  42.5 2.2 %copy-start = (f32[2,64]{1,0:T(2,128)S(1)}, f32[2,64]{1,0:T(2,128)}, u32[]{:S(2)}) copy-start(f32[2,64]{1,0:T(2,128)} %get-tuple-element.7) | copy-start | bytes 1540

commit v3 on v2

--- a/solution.py
+++ b/solution.py
@@ -33,8 +33,14 @@
     return jnp.sum(block, axis=0, keepdims=True)
 
 
+def stripe_groups(blocks):
+    edges = sorted({0, blocks // 2, 3 * blocks // 4, blocks - 1, blocks})
+    return tuple(zip(edges[:-1], edges[1:]))
+
+
 def kernel(
     count,
+    groups,
     scale,
     vr_hbm,
     vi_hbm,
@@ -100,12 +106,14 @@
     load_model.start()
     pl.semaphore_wait(barrier, count - 1)
 
-    def volt_copy(step):
+    def volt_copy(step, group):
+        first, last = groups[group]
+        cols = slice(first * LANES, last * LANES)
         return pltpu.make_async_remote_copy(
-            src_ref=outgoing.at[step],
-            dst_ref=volts.at[step],
-            send_sem=send_sem.at[step],
-            recv_sem=recv_sem.at[step],
+            src_ref=outgoing.at[step, :, cols],
+            dst_ref=volts.at[step, :, cols],
+            send_sem=send_sem.at[group, step],
+            recv_sem=recv_sem.at[group, step],
             device_id={"chan": partner_of(me, step, count)},
             device_id_type=pl.DeviceIdType.MESH,
         )
@@ -114,15 +122,17 @@
         rows = ints[which, lane, pl.ds(channel, samples, stride=count), :]
         return rows.astype(F32).astype(BF16)
 
-    @pl.loop(0, count - 1)
-    def _(turn):
-        step = count - 1 - turn
-        channel = partner_of(me, step, count)
-        for lane in range(blocks):
-            cols = slice(lane * LANES, (lane + 1) * LANES)
-            outgoing[step, 0:samples, cols] = short_rows(0, channel, lane)
-            outgoing[step, samples : 2 * samples, cols] = short_rows(1, channel, lane)
-        volt_copy(step).start()
+    for group, (first, last) in enumerate(groups):
+
+        @pl.loop(0, count - 1)
+        def _(turn):
+            step = count - 1 - turn
+            channel = partner_of(me, step, count)
+            for lane in range(first, last):
+                cols = slice(lane * LANES, (lane + 1) * LANES)
+                outgoing[step, 0:samples, cols] = short_rows(0, channel, lane)
+                outgoing[step, samples : 2 * samples, cols] = short_rows(1, channel, lane)
+            volt_copy(step, group).start()
 
     for lane in range(blocks):
         cols = slice(lane * LANES, (lane + 1) * LANES)
@@ -166,39 +176,42 @@
 
         geom_all[p] = column_sum(row_acc[0].T)
 
-    def gather_products(first, last):
-        @pl.loop(max(first, 1), last)
+    def finish_stripes(group):
+        first, last = groups[group]
+        cols = slice(first * LANES, last * LANES)
+
+        @pl.loop(1, count)
         def _(step):
-            volt_copy(step).wait_recv()
-
-        @pl.loop(first, last)
+            volt_copy(step, group).wait_recv()
+
+        @pl.loop(0, count)
         def _(step):
-            swapped[step, 0:samples, :] = -volts[step, samples : 2 * samples, :]
-            swapped[step, samples : 2 * samples, :] = volts[step, 0:samples, :]
-
-        depth = (last - first) * 2 * samples
-        wide = 2 * LANES
-        for pair in range(blocks // 2):
-            left = volts[first:last, :, pair * wide : (pair + 1) * wide].reshape(depth, wide)
-            for tile in range(pair + 1):
+            swapped[step, 0:samples, cols] = -volts[step, samples : 2 * samples, cols]
+            swapped[step, samples : 2 * samples, cols] = volts[step, 0:samples, cols]
+
+        depth = 2 * samples * count
+        start = first
+        while start < last:
+            stop = min(start + 2, last)
+            span = (stop - start) * LANES
+            left = volts[:, :, start * LANES : stop * LANES].reshape(depth, span)
+            for tile in range(0, stop, 2):
+                end = min(tile + 2, stop)
                 for part, source in ((0, volts), (1, swapped)):
-                    right = source[first:last, :, tile * wide : (tile + 1) * wide].reshape(depth, wide)
+                    right = source[:, :, tile * LANES : end * LANES].reshape(depth, (end - tile) * LANES)
                     product = scale * lax.dot_general(
                         left, right, (((0,), (0,)), ((), ())), preferred_element_type=F32
                     )
-                    for half in range(2):
-                        stripe = 2 * pair + half
-                        offset = stripe * (stripe + 1) // 2 * LANES + tile * wide
-                        width = min(wide, (stripe + 1) * LANES - tile * wide)
-                        res_ref[0, part, :, offset : offset + width] += product[
-                            half * LANES : (half + 1) * LANES, :width
-                        ]
-
-    gather_products(0, count // 2)
-    gather_products(count // 2, count)
-
-    @pl.loop(0, blocks)
-    def _(p):
+                    for stripe in range(start, stop):
+                        offset = (stripe * (stripe + 1) // 2 + tile) * LANES
+                        width = (min(end, stripe + 1) - tile) * LANES
+                        top = (stripe - start) * LANES
+                        res_ref[0, part, :, offset : offset + width] += product[top : top + LANES, :width]
+            start = stop
+
+        pl.loop(first, last)(stripe_terms)
+
+    def stripe_terms(p):
         row_acc[...] = jnp.zeros((2, LANES, LANES), F32)
         rows = lane_block(p)
 
@@ -225,6 +238,9 @@
         terms[p, 2:3] = jnp.full((1, LANES), band * band, F32)
         terms[p, 3:8] = jnp.zeros((5, LANES), F32)
 
+    for group in range(len(groups)):
+        finish_stripes(group)
+
     @pl.loop(0, blocks)
     def _(p):
         terms[p, 0:1] += column_sum(col_acc[p, 0])
@@ -250,7 +266,8 @@
 
     @pl.loop(1, count)
     def _(step):
-        volt_copy(step).wait_send()
+        for group in range(len(groups)):
+            volt_copy(step, group).wait_send()
         term_copy(step).wait()
 
     total = jnp.sum(incoming[...], axis=0)
@@ -269,10 +286,11 @@
     scale = 1.0 / (4096.0 * samples * count)
     blocks = inputs // LANES
     share = inputs // count
+    groups = stripe_groups(blocks)
     in_hbm = pl.BlockSpec(memory_space=pltpu.HBM)
     in_vmem = pl.BlockSpec(memory_space=pltpu.VMEM)
     return pl.pallas_call(
-        functools.partial(kernel, count, scale),
+        functools.partial(kernel, count, groups, scale),
         out_shape=(
             pltpu.VMEM((1,) + model.shape, F32),
             jax.ShapeDtypeStruct((2, share), F32),
@@ -296,8 +314,8 @@
             pltpu.SemaphoreType.DMA((2, blocks)),
             pltpu.SemaphoreType.DMA,
             pltpu.SemaphoreType.DMA,
-            pltpu.SemaphoreType.DMA((count,)),
-            pltpu.SemaphoreType.DMA((count,)),
+            pltpu.SemaphoreType.DMA((len(groups), count)),
+            pltpu.SemaphoreType.DMA((len(groups), count)),
             pltpu.SemaphoreType.DMA((count,)),
             pltpu.SemaphoreType.DMA((count,)),
         ],

time: 45.4 us -> 43.6 us (0.960)
  Pallas kernels: 41.2 us -> 39.4 us
    pallas_call x1, Pallas kernels: 41.2 us -> 39.4 us  [shards(): pl.pallas_call(functools.partial(kernel, count, groups, scale), out_shape...]
where the time goes in v3:
time: 43.6 us; the launch traced here: 43.4 us
  Pallas kernels  39.4 us (90%)
  local copies, waits for them, and re-layouts  2.75 us (6%)
  between operations  1.29 us (3%)
    pallas_call x1, Pallas kernels, shards(): pl.pallas_call(functools.partial(kernel, count, groups, scale), out_shape...  39.4 us
    unnamed x4, local copies, waits for them, and re-layouts  2.75 us

profile of v3, /device:TPU:0, one launch (start us, length us, event | category | flops | bytes accessed | tf_op | source)
XLA Modules:
  0.0 43.4 jit_solution(10099588936314930627)
XLA Ops:
  1.3 39.4 %shard_map.68 = (f32[1,2,128,4608]{3,2,1,0:T(8,128)S(1)}, f32[2,64]{1,0:T(2,128)}) custom-call(s32[256,1024]{1,0:T(8,128)} %bitcast.2, s32[256,1024]{1,0:T(8,128)} %bitcast.3, bf16[2,128,4608]{2,1,0:T(8,128)(2,1)} %model_hbm.1, f32[2,1024]{1,0:T(2,128)} %gain_hbm.1, f32[1]{0:T(128)S(6)} %copy.10.band_ref), custom_call_target="tpu_custom_call" | custom-call | flops 1073741824 | bytes 10485760 | tf_op jit(solution)/shard_map/pallas_call | solution.py:292
  40.7 0.0 copy-start
  40.7 2.2 %copy.9 = f32[1,2,128,4608]{3,2,1,0:T(8,128)} copy(f32[1,2,128,4608]{3,2,1,0:T(8,128)S(1)} %get-tuple-element.2) | data formatting | bytes 9437184
  42.9 0.0 copy-done
  42.9 0.6 %copy.11 = f32[2,64]{1,0:T(2,128)} copy(f32[2,64]{1,0:T(2,128)S(1)} %copy-done) | data formatting | bytes 1024
Async XLA Ops:
  40.7 2.2 %copy-start = (f32[2,64]{1,0:T(2,128)S(1)}, f32[2,64]{1,0:T(2,128)}, u32[]{:S(2)}) copy-start(f32[2,64]{1,0:T(2,128)} %get-tuple-element.7) | copy-start | bytes 1540
